TPU v7x, 512 devices: a whole 4x8x8 slice. The times are simulated.
512 devices in a mesh: view: 16 (over y_lo, z), frame: 32 (over y_hi, x, core).
Axes of the slice: x: 4, y: 8 (y_hi: 4, y_lo: 2; y = y_hi * 2 + y_lo), z: 8, core: 2. Of those that a mesh axis runs over, the one named last changes fastest.
Arguments:
- latents: bfloat16 [16, 64, 256, 640], P('view', 'frame'), may hold values from -12 to 12
- norm_gain: float32 [640], replicated, may hold values from 0.25 to 1.75
- qkv_weight: bfloat16 [640, 1920], P('frame'), may hold values from -10 to 10, as said below
- out_weight: bfloat16 [640, 640], P('frame'), may hold values from -0.25 to 0.25
- conv_weight: bfloat16 [3, 640, 640], P(None, 'frame'), may hold values from -0.125 to 0.125
- view_slope: float32 [10], replicated, may hold values from 0.05 to 1.5
Outputs:
- output: bfloat16 [16, 64, 256, 640], P('view', 'frame')
Inputs may be any that keep to these rules, and one draw needn't show every extreme that they name: `qkv_weight`: query, key and value columns lie side by side in that order.
All inputs are finite; a program needn't handle non-finite values.
Results may differ from a plain program's by a relative error of at most 0.0095.
Values may be sent and summed in bfloat16 or wider, within the bound.
A program may use at most 128 MiB of HBM per device.

v0:
```python
import jax
import jax.numpy as jnp
from jax import lax
from jax.sharding import PartitionSpec as P


def extended(block, sides, width):
    for axis, dim in sides:
        count = lax.axis_size(axis)
        forward = [(i, i + 1) for i in range(count - 1)]
        backward = [(target, source) for source, target in forward]
        low = lax.ppermute(
            lax.slice_in_dim(block, block.shape[dim] - width, None, axis=dim), axis, forward
        )
        high = lax.ppermute(lax.slice_in_dim(block, 0, width, axis=dim), axis, backward)
        block = jnp.concatenate([low, block, high], axis=dim)
    return block


def attend(query, keys, values, dist, view_slope):
    depth = query.shape[-1]
    scores = jnp.einsum("afphd,bfphd->fphab", query, keys, preferred_element_type=jnp.float32) * (
        1.0 / depth**0.5
    )
    scores = scores - view_slope[:, None, None] * dist
    weights = jax.nn.softmax(scores, axis=-1).astype(jnp.bfloat16)
    mixed = jnp.einsum(
        "fphab,bfphd->afphd", weights, values, preferred_element_type=jnp.float32
    ).astype(jnp.bfloat16)
    return mixed.reshape(mixed.shape[0], mixed.shape[1], mixed.shape[2], -1)


def split_heads(block, heads):
    width = block.shape[-1] // 3
    shape = block.shape[:-1] + (heads, width // heads)
    return (
        block[..., :width].reshape(shape),
        block[..., width : 2 * width].reshape(shape),
        block[..., 2 * width :].reshape(shape),
    )


def normalize(block, norm_gain):
    wide = block.astype(jnp.float32)
    return (
        wide * lax.rsqrt(jnp.mean(wide * wide, axis=-1, keepdims=True) + 1e-06) * norm_gain
    ).astype(jnp.bfloat16)


def project_qkv(normed, qkv_weight):
    return jnp.einsum(
        "vfpc,cd->vfpd",
        normed,
        lax.all_gather(qkv_weight, "frame", axis=0, tiled=True),
        preferred_element_type=jnp.float32,
    ).astype(jnp.bfloat16)


def finish(block, mixed, out_weight):
    wide = block.astype(jnp.float32)
    projected = jnp.einsum(
        "vfpc,cd->vfpd",
        mixed,
        lax.all_gather(out_weight, "frame", axis=0, tiled=True),
        preferred_element_type=jnp.float32,
    )
    return (wide + projected).astype(jnp.bfloat16)


def per_device(latents, norm_gain, qkv_weight, out_weight, conv_weight, view_slope):
    views = lax.axis_size("view")
    frames = latents.shape[1]
    heads = view_slope.shape[0]
    order = jnp.arange(views, dtype=jnp.int32)
    normed = normalize(latents, norm_gain)
    qkv = project_qkv(normed, qkv_weight)
    query, keys, values = split_heads(qkv, heads)
    all_keys, all_values = (
        lax.all_gather(keys, "view", axis=0, tiled=True),
        lax.all_gather(values, "view", axis=0, tiled=True),
    )
    gap = jnp.abs(lax.axis_index("view") - order)[None, :]
    dist = jnp.minimum(gap, views - gap).astype(jnp.float32)
    mixed = attend(query, all_keys, all_values, dist, view_slope)
    hidden = finish(latents, mixed, out_weight)
    padded = extended(hidden, (("frame", 1),), 1)
    total = jnp.zeros(hidden.shape, jnp.float32)
    piece = lax.all_gather(conv_weight, "frame", axis=1, tiled=True)
    for tap in range(3):
        columns = padded[:, tap : tap + frames]
        total = total + jnp.einsum(
            "vfpc,cd->vfpd", columns, piece[tap], preferred_element_type=jnp.float32
        )
    return (hidden.astype(jnp.float32) + total).astype(jnp.bfloat16)


def solution(mesh):
    in_specs = (
        P("view", "frame", None, None),
        P(),
        P("frame", None),
        P("frame", None),
        P(None, "frame", None),
        P(),
    )
    out_specs = P("view", "frame", None, None)
    return jax.shard_map(
        per_device, mesh=mesh, in_specs=in_specs, out_specs=out_specs, check_vma=False
    )
```

profile of v0, /device:TPU:1, one launch (start us, length us, event | category | flops | bytes accessed | tf_op | source)
XLA Modules:
  0.0 422.9 jit_solution(10250035226480306337)
XLA Ops:
  6.5 0.7 all-gather.13.cloned.1.call-update
  7.3 1.3 fusion.8
  8.6 69.8 %all-gather.13.cloned.1.call-done = bf16[32,20,1920]{2,1,0:T(8,128)(2,1)} async-done(((bf16[1,20,1920]{2,1,0:T(8,128)(2,1)}), bf16[32,20,1920]{2,1,0:T(8,128)(2,1)}) %all-gather.13.cloned.1.call-update) | async-done | bytes 2457616 | tf_op jit(solution)/shard_map/all_gather | solution.py:54
  78.4 2.8 reshape.134
  81.2 1.8 fusion.2
  83.2 1.1 copy.21
  84.4 1.1 copy.19
  85.6 0.7 copy.23
  86.3 49.0 %all-gather.1 = bf16[32,20,640]{2,1,0:T(8,128)(2,1)S(1)} all-gather(bf16[1,20,640]{2,1,0:T(8,128)(2,1)S(1)} %bitcast.56), channel_id=1, replica_groups=mesh['view'=16,'frame'=32] {'frame'}, dimensions={0}, use_global_device_ids=true | all-gather | bytes 844800 | tf_op jit(solution)/shard_map/all_gather | solution.py:64
  135.6 0.2 copy.20
  136.0 78.5 %all-gather.9.cloned.1.call-done = bf16[16,2,256,10,64]{2,4,3,1,0:T(8,128)(2,1)} async-done(((bf16[1,2,256,10,64]{2,4,3,1,0:T(8,128)(2,1)}), bf16[16,2,256,10,64]{2,4,3,1,0:T(8,128)(2,1)}) %all-gather.9.cloned.1.call-update) | async-done | bytes 10485776 | tf_op jit(solution)/shard_map/all_gather | solution.py:79
  214.5 8.1 %multiply_reduce_fusion.1 = f32[2,256,10,16]{1,2,0,3:T(8,128)S(1)} fusion(f32[2,256,10,64]{1,3,2,0:T(8,128)S(1)} %convert, bf16[16,2,256,10,64]{2,4,3,1,0:T(8,128)(2,1)} %all-gather.9.cloned.1.call-done), kind=kLoop, calls=%fused_computation.3 | loop fusion | flops 15646720 | bytes 12124160
  222.6 0.3 fusion.15
  223.1 113.9 %all-gather.7.cloned.1.call-done = bf16[16,2,256,10,64]{2,4,3,1,0:T(8,128)(2,1)} async-done(((bf16[1,2,256,10,64]{2,4,3,1,0:T(8,128)(2,1)}), bf16[16,2,256,10,64]{2,4,3,1,0:T(8,128)(2,1)}) %all-gather.7.cloned.1.call-update) | async-done | bytes 10485776 | tf_op jit(solution)/shard_map/all_gather | solution.py:80
  337.0 6.8 %multiply_reduce_fusion = bf16[2,256,10,64]{1,3,2,0:T(8,128)(2,1)S(1)} fusion(f32[2,256,10,16]{1,2,0,3:T(8,128)S(1)} %copy.45, bf16[16,2,256,10,64]{2,4,3,1,0:T(8,128)(2,1)} %all-gather.7.cloned.1.call-done), kind=kLoop, calls=%fused_computation.2 | loop fusion | flops 15400960 | bytes 11468800 | tf_op jit(solution)/shard_map/fphab,bfphd->afphd/dot_general | solution.py:27
  343.8 0.8 fusion.7
  344.7 2.6 collective-permute-start.1
  347.2 53.3 %all-gather.11.cloned.1.call-done = bf16[3,640,640]{2,0,1:T(4,128)(2,1)} async-done(((bf16[3,20,640]{2,0,1:T(4,128)(2,1)}), bf16[3,640,640]{2,0,1:T(4,128)(2,1)}) %all-gather.11.cloned.1.call-update) | async-done | bytes 2457616 | tf_op jit(solution)/shard_map/all_gather | solution.py:88
  400.6 8.1 %fusion.43 = (bf16[1,640,640]{2,0,1:T(2,128)(2,1)S(1)}, bf16[1,640,640]{2,0,1:T(2,128)(2,1)S(1)}, bf16[1,640,640]{2,0,1:T(2,128)(2,1)S(1)}) fusion(bf16[3,640,640]{2,0,1:T(4,128)(2,1)} %all-gather.11.cloned.1.call-done), kind=kLoop, calls=%fused_computation.53 | loop fusion | bytes 4915200 | tf_op jit(solution)/shard_map/slice | solution.py:92
  408.7 2.0 collective-permute-start
  410.7 0.8 fusion.17
  411.5 0.8 fusion.16
  412.3 2.5 collective-permute-done
  414.7 1.7 fusion.6
  (28 shorter events, 1.0 us)
Async XLA Ops:
  6.5 71.9 %all-gather.13.cloned.1.call-start = ((), (), s32[]{:S(2)}) async-start(), calls=%async_computation.3 | async-start | bytes 3041280 | tf_op jit(solution)/shard_map/all_gather | solution.py:54
  7.3 207.3 %all-gather.9.cloned.1.call-start = ((), (), s32[]{:S(2)}) async-start(), calls=%async_computation.1 | async-start | bytes 11141120 | tf_op jit(solution)/shard_map/all_gather | solution.py:79
  8.6 72.6 %copy-start = (bf16[1,2,256,640]{3,2,1,0:T(8,128)(2,1)S(1)}, bf16[1,2,256,640]{3,2,1,0:T(8,128)(2,1)}, u32[]{:S(2)}) copy-start(bf16[1,2,256,640]{3,2,1,0:T(8,128)(2,1)} %param.6) | copy-start | bytes 1966084
  8.6 72.6 %copy-start.5 = (f32[640]{0:T(1024)S(1)}, f32[640]{0:T(1024)}, u32[]{:S(2)}) copy-start(f32[640]{0:T(1024)} %param.7) | copy-start | bytes 7684
  84.3 1.3 copy-start.2
  84.3 2.0 copy-start.3
  84.4 252.7 %all-gather.7.cloned.1.call-start = ((), (), s32[]{:S(2)}) async-start(), calls=%async_computation | async-start | bytes 11141120 | tf_op jit(solution)/shard_map/all_gather | solution.py:80
  85.5 50.0 %copy-start.4 = (f32[10]{0:T(128)S(1)}, f32[10]{0:T(128)}, u32[]{:S(2)}) copy-start(f32[10]{0:T(128)} %param.11) | copy-start | bytes 124
  85.5 315.0 %all-gather.11.cloned.1.call-start = ((), (), s32[]{:S(2)}) async-start(), calls=%async_computation.2 | async-start | bytes 3379200 | tf_op jit(solution)/shard_map/all_gather | solution.py:88
  223.1 120.7 %copy-start.1 = (bf16[1,2,256,640]{3,2,1,0:T(8,128)(2,1)S(1)}, bf16[1,2,256,640]{3,2,1,0:T(8,128)(2,1)}, u32[]{:S(2)}) copy-start(bf16[1,2,256,640]{3,2,1,0:T(8,128)(2,1)} %param.6) | copy-start | bytes 1966084
  344.7 66.8 %collective-permute-start.1 = (bf16[1,1,256,640]{3,2,1,0:T(8,128)(2,1)S(1)}, bf16[1,1,256,640]{3,2,1,0:T(8,128)(2,1)S(1)}, u32[]{:S(2)}, u32[]{:S(2)}) collective-permute-start(bf16[1,1,256,640]{3,2,1,0:T(8,128)(2,1)S(1)} %get-tuple-element.12), channel_id=1, source_target_pairs={{1,0},{2,1},{3,2},{4,3},{5,4},{6,5},{7,6},{8,7},{9,8},{10,9},{11,1... | collective-permute-start | bytes 983048 | tf_op jit(solution)/shard_map/ppermute | solution.py:15
  408.7 6.0 %collective-permute-start = (bf16[1,1,256,640]{3,2,1,0:T(8,128)(2,1)S(1)}, bf16[1,1,256,640]{3,2,1,0:T(8,128)(2,1)S(1)}, u32[]{:S(2)}, u32[]{:S(2)}) collective-permute-start(bf16[1,1,256,640]{3,2,1,0:T(8,128)(2,1)S(1)} %get-tuple-element.11), channel_id=1, source_target_pairs={{0,1},{1,2},{2,3},{3,4},{4,5},{5,6},{6,7},{7,8},{8,9},{9,10},{10,1... | collective-permute-start | bytes 983048 | tf_op jit(solution)/shard_map/ppermute | solution.py:12
Sparse Core Ops, SparseCore 0:
  10.6 67.8 all-gather.12
  84.5 129.9 all-gather.8
  216.6 120.3 all-gather.6
  340.1 60.4 all-gather.10
where the time goes:
time: 429 us; the launch traced here: 423 us
  waiting for transfers between devices  319 us (74%)
  blocking collectives  49 us (11%)
  other arithmetic  16.6 us (4%)
  local copies, waits for them, and re-layouts  14.7 us (3%)
  between operations  13.4 us (3%)
  matrix products  5.79 us (1%)
  starting transfers between devices  4.72 us (1%)
    all_gather x1, waiting for transfers between devices, per_device(): lax.all_gather(values, 'view', axis=0, tiled=True)  114 us
    all_gather x1, waiting for transfers between devices, per_device(): lax.all_gather(keys, 'view', axis=0, tiled=True)  78.5 us
    all_gather x1, waiting for transfers between devices, project_qkv(): lax.all_gather(qkv_weight, 'frame', axis=0, tiled=True)  69.8 us
    all_gather x1, waiting for transfers between devices, per_device(): piece = lax.all_gather(conv_weight, 'frame', axis=1, tiled=True)  53.3 us
    all_gather x1, blocking collectives, finish(): lax.all_gather(out_weight, 'frame', axis=0, tiled=True)  49 us
  transfers between devices with their start and end apart: 6, of which 5 were waited for; matrix products, arithmetic and copies ran while one was open for 7% of the time, Pallas kernels for 0%

commit v1 on v0

v1 whole, which is shorter than its diff:
```python
import functools

import jax
import jax.numpy as jnp
from jax import lax
from jax.experimental import pallas as pl
from jax.experimental.pallas import tpu as pltpu
from jax.sharding import PartitionSpec as P

ZS, YLS, XS, YHS = 8, 2, 4, 4
VIEWS, PIX, C, HEADS = 16, 256, 640, 10
ROWS = 80
QW, OW = 512, 640
PEERS = [(dy, dz) for dz in (4, 3, 5, 2, 6, 1, 7, 0) for dy in (0, 1) if (dy, dz) != (0, 0)]
XSTEPS = (1, -1, 2)
XFROM = (3, 1, 2)
ORDER = (0, 1, 3, 2)
BF, F32 = jnp.bfloat16, jnp.float32


class Place:
    def __init__(self):
        v, f = lax.axis_index("view"), lax.axis_index("frame")
        self.view, self.frame = v, f
        self.yl, self.z = v // ZS, v % ZS
        self.yh, self.x, self.core = f // (XS * 2), (f // 2) % XS, f % 2
        self.even = self.yl == 0
        self.odd = self.yl == 1

    def at(self, yl, z, yh, x, core):
        return (yl * ZS + z, yh * (XS * 2) + x * 2 + core)

    def x_peer(self, d):
        return (self.view, self.yh * (XS * 2) + ((self.x + d + XS) % XS) * 2 + self.core)

    def y_peer(self, d):
        y = (self.yh * 2 + self.yl + d + 8) % 8
        return self.at(y % 2, self.z, y // 2, self.x, self.core)

    def sibling(self):
        return (self.view, self.yh * (XS * 2) + self.x * 2 + 1 - self.core)

    def frame_peer(self, d):
        return (self.view, (self.frame + d + 32) % 32)

    def view_peer(self, dy, dz):
        view = ((self.yl + dy) % YLS) * ZS + (self.z + dz) % ZS
        return view, (view, self.frame)


def remote(src, dst, send, recv, device):
    return pltpu.make_async_remote_copy(
        src_ref=src, dst_ref=dst, send_sem=send, recv_sem=recv,
        device_id=device, device_id_type=pl.DeviceIdType.MESH,
    )


class GatherXY:
    def __init__(self, here, buf, stride, off, n, sems):
        self.h, self.buf, self.stride, self.off, self.n = here, buf, stride, off, n
        (self.xs, self.xr, self.rs, self.rr, self.ls, self.lr, self.ss, self.sr) = sems

    def piece(self, b, rel):
        h = self.h
        row = pl.multiple_of(((b % YHS) * 2 + h.core) * ROWS, 16)
        col = pl.multiple_of(((h.x + rel) % XS) * self.stride + self.off, 128)
        return self.buf.at[pl.ds(row, ROWS), pl.ds(col, self.n)]

    def copy(self, b, rel, send, recv, device):
        p = self.piece(b, rel)
        return remote(p, p, send, recv, device)

    def to_sibling(self, b, rel):
        i = (b % YHS) * XS + (self.h.x + rel) % XS
        self.copy(b, rel, self.ss.at[i], self.sr.at[i], self.h.sibling()).start()

    def right(self, i, b, rel):
        return self.copy(b, rel, self.rs.at[i], self.rr.at[i], self.h.y_peer(1))

    def left(self, i, b, rel):
        return self.copy(b, rel, self.ls.at[i], self.lr.at[i], self.h.y_peer(-1))

    def steps(self):
        h = self.h
        for i, d in enumerate(XSTEPS):
            self.copy(h.yh, 0, self.xs.at[i], self.xr.at[i], h.x_peer(d)).start()
        for p, rel in enumerate(ORDER):
            if p:
                i = XFROM.index(rel)
                self.copy(h.yh, rel, self.xs.at[i], self.xr.at[i], h.x_peer(1)).wait_recv()

            @pl.when(h.odd)
            def _():
                self.right(p, h.yh, rel).start()

            @pl.when(h.even)
            def _():
                self.left(p, h.yh, rel).start()

            self.to_sibling(h.yh, rel)
            if p == 0:
                yield
        yield
        for i in range(6):
            far = i >= 4
            rel = ORDER[i - 4] if far else ORDER[i]
            b = h.yh + (2 if far else 3)
            self.right(i, b, rel).wait_recv()

            @pl.when(h.even)
            def _():
                self.right(i, b, rel).start()

            if i < 2:
                @pl.when(h.odd)
                def _():
                    self.right(4 + i, b, rel).start()

            self.to_sibling(b, rel)

            rel = ORDER[i - 2] if far else ORDER[i]
            b = h.yh + (2 if far else 1)
            self.left(i, b, rel).wait_recv()

            @pl.when(h.odd)
            def _():
                self.left(i, b, rel).start()

            if 2 <= i < 4:
                @pl.when(h.even)
                def _():
                    self.left(2 + i, b, rel).start()

            self.to_sibling(b, rel)
            yield

    def arrive(self):
        for i in range(16):
            self.copy(0, 0, self.ss.at[i], self.sr.at[i], self.h.sibling()).wait_recv()

    def drain(self):
        for sem, count in ((self.xs, 3), (self.rs, 6), (self.ls, 6), (self.ss, 16)):
            for i in range(count):
                self.copy(0, 0, sem.at[i], self.xr.at[0], self.h.sibling()).wait_send()

    @staticmethod
    def sems():
        return [pltpu.SemaphoreType.DMA((k,)) for k in (3, 3, 6, 6, 6, 6, 16, 16)]


class GatherYX:
    def __init__(self, here, buf, stride, off, n, first, sems):
        self.h, self.buf, self.stride, self.off, self.n = here, buf, stride, off, n
        self.first = first
        (self.rs, self.rr, self.ls, self.lr, self.xs, self.xr, self.ss, self.sr) = sems

    def piece(self, b, rel, part=0):
        h = self.h
        row = pl.multiple_of(((b % YHS) * 2 + h.core) * ROWS, 16)
        off = self.off + (self.first if part == 2 else 0)
        n = (self.n, self.first, self.n - self.first)[part]
        col = pl.multiple_of(((h.x + rel) % XS) * self.stride + off, 128)
        return self.buf.at[pl.ds(row, ROWS), pl.ds(col, n)]

    def copy(self, b, rel, send, recv, device, part=0):
        p = self.piece(b, rel, part)
        return remote(p, p, send, recv, device)

    def to_sibling(self, b, rel):
        i = (b % YHS) * XS + (self.h.x + rel) % XS
        self.copy(b, rel, self.ss.at[i], self.sr.at[i], self.h.sibling()).start()

    def right(self, i, b):
        part = 1 if i else 0
        return self.copy(b, 0, self.rs.at[i], self.rr.at[i], self.h.y_peer(1), part)

    def left(self, i, b):
        part = 2 if i else 0
        return self.copy(b, 0, self.ls.at[i], self.lr.at[i], self.h.y_peer(-1), part)

    def across(self, j, b):
        for i, d in enumerate(XSTEPS):
            k = j * 3 + i
            self.copy(b, 0, self.xs.at[k], self.xr.at[k], self.h.x_peer(d)).start()
        self.to_sibling(b, 0)

    def steps(self):
        h = self.h

        @pl.when(h.odd)
        def _():
            self.right(0, h.yh).start()

        @pl.when(h.even)
        def _():
            self.left(0, h.yh).start()

        self.across(0, h.yh)
        yield
        b = h.yh + 3
        self.right(0, b).wait_recv()

        @pl.when(h.even)
        def _():
            self.right(0, b).start()

        @pl.when(h.odd)
        def _():
            self.right(1, b).start()

        self.across(1, b)
        b = h.yh + 1
        self.left(0, b).wait_recv()

        @pl.when(h.odd)
        def _():
            self.left(0, b).start()

        @pl.when(h.even)
        def _():
            self.left(1, b).start()

        self.across(2, b)
        yield
        b = h.yh + 2
        self.right(1, b).wait_recv()

        @pl.when(h.even)
        def _():
            self.right(1, b).start()

        self.left(1, b).wait_recv()

        @pl.when(h.odd)
        def _():
            self.left(1, b).start()

        self.across(3, b)
        yield
        for j, step in enumerate((0, 3, 1, 2)):
            for i, rel in enumerate(XFROM):
                k = j * 3 + i
                self.copy(h.yh + step, rel, self.xs.at[k], self.xr.at[k], h.x_peer(1)).wait_recv()
                self.to_sibling(h.yh + step, rel)
            yield

    def arrive(self):
        for i in range(16):
            self.copy(0, 0, self.ss.at[i], self.sr.at[i], self.h.sibling()).wait_recv()

    def drain(self):
        for i in range(2):
            self.right(i, 0).wait_send()
            self.left(i, 0).wait_send()
        for sem, count in ((self.xs, 12), (self.ss, 16)):
            for i in range(count):
                self.copy(0, 0, sem.at[i], self.xr.at[0], self.h.sibling()).wait_send()

    @staticmethod
    def sems():
        return [pltpu.SemaphoreType.DMA((k,)) for k in (2, 2, 2, 2, 12, 12, 16, 16)]


def advance(*generators, times=1):
    for _ in range(times):
        for g in generators:
            next(g, None)


def kernel(
    lat, gain, qsh, osh, csh, slope, out,
    pieces, xin, outb, back, dist, wq, wo, sq, so, r1q, r1o, r32, qkv, mix, hid,
    hsend, hleft, hright,
    in_s, in_r, out_s, out_r, halo_s, halo_r, s1_s, s1_r, *sems,
):
    h = Place()
    barrier = pltpu.get_barrier_semaphore()
    partners = [h.view_peer(*p)[1] for p in PEERS]
    for dx in range(XS):
        for dc in range(2):
            if dx or dc:
                partners.append(
                    (h.view, h.yh * 8 + ((h.x + dx) % XS) * 2 + (h.core + dc) % 2)
                )
    partners += [h.y_peer(1), h.y_peer(-1), h.frame_peer(1), h.frame_peer(-1)]
    for p in partners:
        pl.semaphore_signal(barrier, inc=1, device_id=p, device_id_type=pl.DeviceIdType.MESH)

    sq[...] = jnp.zeros_like(sq)
    so[...] = jnp.zeros_like(so)
    sq[0:20, 0:1920] = qsh[...]
    so[0:20, 0:640] = osh[...]
    for t in range(3):
        so[0:20, 640 * (t + 1) : 640 * (t + 2)] = csh[t]
    both = [lat[0, f].astype(F32).reshape(32, 8, C) for f in range(2)]
    pieces[...] = jnp.stack(both, axis=1).reshape(32, 16, C).astype(BF)
    row = lax.broadcasted_iota(jnp.int32, (256, 256), 0)
    col = lax.broadcasted_iota(jnp.int32, (256, 256), 1)
    gap = jnp.abs(row // 16 - col // 16)
    gap = jnp.minimum(gap, VIEWS - gap).astype(F32)
    dist[...] = jnp.where(row % 16 == col % 16, gap, 1e30)

    pl.semaphore_wait(barrier, len(partners))

    half = h.x // 2
    slot = (h.x % 2) * 2 + h.core
    stages = ((sq, r1q, QW), (so, r1o, OW))

    def shard(t, x):
        src, dst, width = stages[t]
        device = (h.view, h.yh * 8 + x * 2 + half)
        return remote(
            src.at[:, pl.ds(x * width, width)], dst.at[slot], s1_s.at[t, x], s1_r.at[t, slot], device
        )

    mine = half == h.core
    for t in range(2):
        for x in range(XS):
            src, dst, width = stages[t]

            @pl.when(jnp.logical_not(mine & (h.x == x)))
            def _():
                shard(t, x).start()

            @pl.when(mine & (h.x == x))
            def _():
                pltpu.make_async_copy(
                    src.at[:, pl.ds(x * width, width)], dst.at[slot], s1_r.at[t, slot]
                ).start()

    def send_in(c, i):
        v, device = h.view_peer(*PEERS[i])
        return remote(
            pieces.at[v * 2 + c], xin.at[c, h.view], in_s.at[c, i], in_r.at[c, i], device
        )

    for c in range(2):
        for i in range(15):
            send_in(c, i).start()
        xin[c, h.view] = pieces[h.view * 2 + c]

    def put_together(t):
        src, dst, width = stages[t]
        for s in range(4):
            pltpu.make_async_copy(dst.at[s], dst.at[s], s1_r.at[t, s]).wait()
            r32[20 * s : 20 * s + 20, 0:width] = dst[s, 0:20, :].astype(F32)
        buf = (wq, wo)[t]
        rows = pl.multiple_of((h.yh * 2 + h.core) * ROWS, 16)
        cols = pl.multiple_of(h.x * width, 128)
        buf[pl.ds(rows, ROWS), pl.ds(cols, width)] = r32[:, 0:width].astype(BF)

    qa = GatherXY(h, wq, QW, 0, 256, sems[0:8])
    qb = GatherYX(h, wq, QW, 256, 256, 128, sems[8:16])
    oa = GatherXY(h, wo, OW, 0, 384, sems[16:24])
    ob = GatherYX(h, wo, OW, 384, 256, 128, sems[24:32])
    sqa, sqb, soa, sob = qa.steps(), qb.steps(), oa.steps(), ob.steps()

    put_together(0)
    advance(sqa, sqb, times=2)
    put_together(1)
    advance(sqa, sqb, times=3)
    advance(soa, sob)
    advance(sqa, sqb, times=8)
    qa.arrive()
    qb.arrive()

    def project(c):
        for i in range(15):
            send_in(c, i).wait_recv()
        wide = xin[c].reshape(256, C).astype(F32)
        scale = lax.rsqrt(jnp.mean(wide * wide, axis=-1, keepdims=True) + 1e-06)
        normed = (wide * scale * gain[...]).astype(BF)
        for t in range(5):
            qkv[c, :, 384 * t : 384 * (t + 1)] = jnp.dot(
                normed, wq[:, 384 * t : 384 * (t + 1)], preferred_element_type=F32
            ).astype(BF)

    low = lax.broadcasted_iota(jnp.int32, (256, 128), 1) < 64

    def attend(c, s):
        q = qkv[c, :, 128 * s : 128 * (s + 1)]
        k = qkv[c, :, 640 + 128 * s : 640 + 128 * (s + 1)]
        v = qkv[c, :, 1280 + 128 * s : 1280 + 128 * (s + 1)]
        v = jnp.concatenate([v, jnp.ones_like(v)], axis=1)
        parts = []
        for e in range(2):
            qe = jnp.where(low if e == 0 else jnp.logical_not(low), q, jnp.zeros_like(q))
            scores = lax.dot_general(
                qe, k, (((1,), (1,)), ((), ())), preferred_element_type=F32
            )
            scores = scores * 0.125 - slope[2 * s + e] * dist[...]
            top = jnp.max(scores, axis=-1, keepdims=True)
            weights = jnp.exp(scores - top).astype(BF)
            o = jnp.dot(weights, v, preferred_element_type=F32)
            parts.append(o[:, 0:128] / o[:, 128:256])
        mix[c, :, 128 * s : 128 * (s + 1)] = jnp.where(low, parts[0], parts[1]).astype(BF)

    def halo(c, side):
        dst = (hright, hleft)[side]
        return remote(
            hsend.at[c, side], dst.at[c], halo_s.at[c, side], halo_r.at[c, side],
            h.frame_peer((-1, 1)[side]),
        )

    def add(c):
        wide = xin[c].reshape(256, C).astype(F32)
        total = wide + jnp.dot(mix[c], wo[:, 0:640], preferred_element_type=F32)
        hidden = total.astype(BF)
        hid[c] = hidden
        split = hidden.astype(F32).reshape(16, 2, 8, C)
        for side in range(2):
            hsend[c, side] = split[:, side].reshape(128, C).astype(BF)
            halo(c, side).start()

    def convolve(c):
        for side in range(2):
            halo(c, side).wait_recv()
        wide = hid[c].astype(F32)
        split = wide.reshape(16, 2, 8, C)
        before = hleft[c].astype(F32).reshape(16, 8, C)
        after = hright[c].astype(F32).reshape(16, 8, C)
        before = jnp.where(h.frame == 0, 0.0, before)
        after = jnp.where(h.frame == 31, 0.0, after)
        taps = (
            jnp.stack([before, split[:, 0]], axis=1).reshape(256, C).astype(BF),
            hid[c],
            jnp.stack([split[:, 1], after], axis=1).reshape(256, C).astype(BF),
        )
        for t in range(3):
            wide = wide + jnp.dot(
                taps[t], wo[:, 640 * (t + 1) : 640 * (t + 2)], preferred_element_type=F32
            )
        outb[c] = wide.astype(BF).reshape(16, 16, C)
        for i in range(15):
            send_out(c, i).start()
        back[c, h.view] = outb[c, h.view]

    def send_out(c, i):
        v, device = h.view_peer(*PEERS[i])
        return remote(
            outb.at[c, v], back.at[c, h.view], out_s.at[c, i], out_r.at[c, i], device
        )

    project(0)
    advance(soa, sob)
    for s in range(5):
        attend(0, s)
        advance(soa, sob)
    advance(soa, sob, times=8)
    oa.arrive()
    ob.arrive()
    add(0)
    project(1)
    attend(1, 0)
    attend(1, 1)
    convolve(0)
    for s in range(2, 5):
        attend(1, s)
    add(1)
    convolve(1)

    for g in (qa, qb, oa, ob):
        g.drain()
    for t in range(2):
        for x in range(XS):
            @pl.when(jnp.logical_not(mine & (h.x == x)))
            def _():
                shard(t, x).wait_send()
    for c in range(2):
        for side in range(2):
            halo(c, side).wait_send()
        for i in range(15):
            send_in(c, i).wait_send()
    for c in range(2):
        for i in range(15):
            send_out(c, i).wait_recv()
    both = [back[c].astype(F32).reshape(16, 2, 8, C) for c in range(2)]
    for f in range(2):
        out[0, f] = jnp.stack([b[:, f] for b in both], axis=1).reshape(PIX, C).astype(BF)
    for c in range(2):
        for i in range(15):
            send_out(c, i).wait_send()


def per_device(latents, norm_gain, qkv_weight, out_weight, conv_weight, view_slope):
    vmem = pl.BlockSpec(memory_space=pltpu.VMEM)
    dma = pltpu.SemaphoreType.DMA
    scratch = [
        pltpu.VMEM((32, 16, C), BF),
        pltpu.VMEM((2, 16, 16, C), BF),
        pltpu.VMEM((2, 16, 16, C), BF),
        pltpu.VMEM((2, 16, 16, C), BF),
        pltpu.VMEM((256, 256), F32),
        pltpu.VMEM((C, 4 * QW), BF),
        pltpu.VMEM((C, 4 * OW), BF),
        pltpu.VMEM((32, 4 * QW), BF),
        pltpu.VMEM((32, 4 * OW), BF),
        pltpu.VMEM((4, 32, QW), BF),
        pltpu.VMEM((4, 32, OW), BF),
        pltpu.VMEM((ROWS, OW), F32),
        pltpu.VMEM((2, 256, 3 * C), BF),
        pltpu.VMEM((2, 256, C), BF),
        pltpu.VMEM((2, 256, C), BF),
        pltpu.VMEM((2, 2, 128, C), BF),
        pltpu.VMEM((2, 128, C), BF),
        pltpu.VMEM((2, 128, C), BF),
        dma((2, 15)), dma((2, 15)), dma((2, 15)), dma((2, 15)),
        dma((2, 2)), dma((2, 2)), dma((2, 4)), dma((2, 4)),
    ]
    scratch += GatherXY.sems() + GatherYX.sems() + GatherXY.sems() + GatherYX.sems()
    return pl.pallas_call(
        kernel,
        out_shape=jax.ShapeDtypeStruct(latents.shape, latents.dtype),
        in_specs=[vmem] * 5 + [pl.BlockSpec(memory_space=pltpu.SMEM)],
        out_specs=vmem,
        scratch_shapes=scratch,
        compiler_params=pltpu.CompilerParams(
            collective_id=0, has_side_effects=True, vmem_limit_bytes=56 * 1024 * 1024
        ),
        cost_estimate=pl.CostEstimate(
            flops=4 * 10**9, bytes_accessed=2 * 10**6, transcendentals=10**6
        ),
    )(latents, norm_gain.reshape(1, C), qkv_weight, out_weight, conv_weight, view_slope)


def solution(mesh):
    in_specs = (
        P("view", "frame", None, None),
        P(),
        P("frame", None),
        P("frame", None),
        P(None, "frame", None),
        P(),
    )
    return jax.shard_map(
        per_device,
        mesh=mesh,
        in_specs=in_specs,
        out_specs=P("view", "frame", None, None),
        check_vma=False,
    )
```

time: 429 us -> 158 us (0.37)
  the two profiles are of different devices: /device:TPU:1 before, /device:TPU:56 now
where the time goes in v1:
time: 158 us
  Pallas kernels  155 us (98%)
  local copies, waits for them, and re-layouts  3.25 us (2%)
    pallas_call x1, Pallas kernels, per_device(): pl.pallas_call(kernel, out_shape=jax.ShapeDtypeStruct(latents.shape, late...  155 us

profile of v1, /device:TPU:56, one launch (start us, length us, event | category | flops | bytes accessed | tf_op | source)
XLA Modules:
  0.0 158.2 jit_solution(993226833444728383)
XLA Ops:
  0.0 1.3 reshape.3.gain
  1.3 155.0 %shard_map.64 = bf16[1,2,256,640]{3,2,1,0:T(8,128)(2,1)} custom-call(bf16[1,2,256,640]{3,2,1,0:T(8,128)(2,1)} %lat.1, f32[1,640]{1,0:T(1,128)} %reshape.3.gain, bf16[20,1920]{1,0:T(8,128)(2,1)} %qsh.1, bf16[20,640]{1,0:T(8,128)(2,1)} %osh.1, bf16[3,20,640]{2,1,0:T(8,128)(2,1)} %csh.1, f32[10]{0:T(128)} %slope.1), custom_call_target="tpu_custom_call" | custom-call | flops 4000000000 | bytes 2000000 | tf_op jit(solution)/shard_map/pallas_call | solution.py:511
  156.2 2.0 %copy.8 = bf16[1,2,256,640]{3,2,1,0:T(8,128)(2,1)} copy(bf16[1,2,256,640]{3,2,1,0:T(8,128)(2,1)} %shard_map.64) | data formatting | bytes 1310720

commit v2 on v1

v2 whole, which is shorter than its diff:
```python
import jax
import jax.numpy as jnp
from jax import lax
from jax.experimental import pallas as pl
from jax.experimental.pallas import tpu as pltpu
from jax.sharding import PartitionSpec as P

ZS, YLS, XS, YHS = 8, 2, 4, 4
VIEWS, PIX, C, HEADS = 16, 256, 640, 10
ROWS = 80
QA, OA, GROUP = 1024, 384, 384
PEERS = [(dy, dz) for dz in (4, 3, 5, 2, 6, 1, 7, 0) for dy in (0, 1) if (dy, dz) != (0, 0)]
XSTEPS = (1, -1, 2)
XFROM = (3, 1, 2)
BF, F32 = jnp.bfloat16, jnp.float32


class Place:
    def __init__(self):
        v, f = lax.axis_index("view"), lax.axis_index("frame")
        self.view, self.frame = v, f
        self.yl, self.z = v // ZS, v % ZS
        self.yh, self.x, self.core = f // (XS * 2), (f // 2) % XS, f % 2
        self.even = self.yl == 0
        self.odd = self.yl == 1

    def at(self, yl, z, yh, x, core):
        return (yl * ZS + z, yh * (XS * 2) + x * 2 + core)

    def x_peer(self, d):
        return (self.view, self.yh * (XS * 2) + ((self.x + d + XS) % XS) * 2 + self.core)

    def y_peer(self, d):
        y = (self.yh * 2 + self.yl + d + 8) % 8
        return self.at(y % 2, self.z, y // 2, self.x, self.core)

    def sibling(self):
        return (self.view, self.yh * (XS * 2) + self.x * 2 + 1 - self.core)

    def frame_peer(self, d):
        return (self.view, (self.frame + d + 32) % 32)

    def view_peer(self, dy, dz):
        view = ((self.yl + dy) % YLS) * ZS + (self.z + dz) % ZS
        return view, (view, self.frame)


def remote(src, dst, send, recv, device):
    return pltpu.make_async_remote_copy(
        src_ref=src, dst_ref=dst, send_sem=send, recv_sem=recv,
        device_id=device, device_id_type=pl.DeviceIdType.MESH,
    )


class Gather:
    def __init__(self, here, buf, across, sems):
        self.h, self.buf, self.across = here, buf, across
        self.count = buf.shape[0]
        self.side = 2 * here.yl - 1
        (self.ys, self.yr, self.xs, self.xr, self.ss, self.sr) = sems

    def piece(self, b, p):
        row = pl.multiple_of((((b + 8) % YHS) * 2 + self.h.core) * ROWS, 16)
        return self.buf.at[p, pl.ds(row, ROWS)]

    def copy(self, b, p, send, recv, device):
        ref = self.piece(b, p)
        return remote(ref, ref, send, recv, device)

    def hop(self, k, i, b, p):
        d = (self.side, -self.side, self.side)[k]
        return self.copy(b, p, self.ys.at[k, i], self.yr.at[k, i], self.h.y_peer(d))

    def to_sibling(self, b, p):
        i = ((b + 8) % YHS) * self.count + p
        self.copy(b, p, self.ss.at[i], self.sr.at[i], self.h.sibling()).start()

    def pass_on(self, k, b, p):
        if self.across:
            for i, d in enumerate(XSTEPS):
                i += 3 * k
                self.copy(b, p, self.xs.at[i], self.xr.at[i], self.h.x_peer(d)).start()
        self.to_sibling(b, p)

    def steps(self):
        h = self.h
        own = [h.x] if self.across else range(self.count)
        blocks = (h.yh + self.side, h.yh - self.side, h.yh + 2)
        for i, p in enumerate(own):
            self.hop(0, i, h.yh, p).start()
        for p in own:
            self.pass_on(0, h.yh, p)
        yield
        for k in range(3):
            for i, p in enumerate(own):
                self.hop(k, i, blocks[k], p).wait_recv()
                if k < 2:
                    self.hop(k + 1, i, blocks[k], p).start()
                self.pass_on(k + 1, blocks[k], p)
            yield
        if self.across:
            for k, b in enumerate((h.yh,) + blocks):
                for i, rel in enumerate(XFROM):
                    p = (h.x + rel) % XS
                    i += 3 * k
                    self.copy(b, p, self.xs.at[i], self.xr.at[i], h.x_peer(1)).wait_recv()
                    self.to_sibling(b, p)
                yield

    def arrive(self):
        for i in range(YHS * self.count):
            self.copy(0, 0, self.ss.at[i], self.sr.at[i], self.h.sibling()).wait_recv()

    def drain(self):
        own = 1 if self.across else self.count
        waits = [self.ys.at[k, i] for k in range(3) for i in range(own)]
        waits += [self.ss.at[i] for i in range(YHS * self.count)]
        if self.across:
            waits += [self.xs.at[i] for i in range(12)]
        for sem in waits:
            self.copy(0, 0, sem, self.sr.at[0], self.h.sibling()).wait_send()

    @staticmethod
    def sems(count, across):
        own = 1 if across else count
        shapes = ((3, own), (3, own), (12,), (12,), (YHS * count,), (YHS * count,))
        return [pltpu.SemaphoreType.DMA(k) for k in shapes]


def advance(*generators, times=1):
    for _ in range(times):
        for g in generators:
            next(g, None)


def kernel(
    lat, gain, qsh, osh, csh, slope, out,
    pieces, xin, outb, back, dist, wqa, wqb, woa, wob, sq, so, r1q, r1o, r32, qkv, mix, hid,
    hsend, hleft, hright,
    in_s, in_r, out_s, out_r, halo_s, halo_r, s1_s, s1_r, *sems,
):
    h = Place()
    barrier = pltpu.get_barrier_semaphore()
    partners = [h.view_peer(*p)[1] for p in PEERS]
    for dx in range(XS):
        for dc in range(2):
            if dx or dc:
                partners.append(
                    (h.view, h.yh * 8 + ((h.x + dx) % XS) * 2 + (h.core + dc) % 2)
                )
    partners += [h.y_peer(1), h.y_peer(-1), h.frame_peer(1), h.frame_peer(-1)]
    for p in partners:
        pl.semaphore_signal(barrier, inc=1, device_id=p, device_id_type=pl.DeviceIdType.MESH)

    for x in range(XS):
        first, last = QA + GROUP * x, QA + GROUP * (x + 1)
        sq[x, 0:20, 0:QA] = qsh[:, 0:QA]
        if first < 1920:
            sq[x, 0:20, QA : QA + min(last, 1920) - first] = qsh[:, first : min(last, 1920)]
        if last > 1920:
            skip = max(first, 1920)
            sq[x, 0:20, QA + skip - first :] = osh[:, skip - 1920 : last - 1920]
        so[x, 0:20, 0:OA] = csh[0, :, 0:OA]
        at, end = OA + GROUP * x, OA + GROUP * (x + 1)
        while at < end:
            t = at // C
            stop = min(end, C * (t + 1))
            to = OA + at - (OA + GROUP * x)
            so[x, 0:20, to : to + stop - at] = csh[t, :, at - C * t : stop - C * t]
            at = stop
        sq[x, 20:32, :] = jnp.zeros((12, QA + GROUP), BF)
        so[x, 20:32, :] = jnp.zeros((12, OA + GROUP), BF)
    both = [lat[0, f].astype(F32).reshape(32, 8, C) for f in range(2)]
    pieces[...] = jnp.stack(both, axis=1).reshape(32, 16, C).astype(BF)
    row = lax.broadcasted_iota(jnp.int32, (256, 256), 0)
    col = lax.broadcasted_iota(jnp.int32, (256, 256), 1)
    gap = jnp.abs(row // 16 - col // 16)
    gap = jnp.minimum(gap, VIEWS - gap).astype(F32)
    dist[...] = jnp.where(row % 16 == col % 16, gap, 1e30)

    pl.semaphore_wait(barrier, len(partners))

    half = h.x // 2
    slot = (h.x % 2) * 2 + h.core
    stages = ((sq, r1q, QA + GROUP), (so, r1o, OA + GROUP))

    def shard(t, x):
        src, dst = stages[t][:2]
        device = (h.view, h.yh * 8 + x * 2 + half)
        return remote(
            src.at[x], dst.at[slot], s1_s.at[t, x], s1_r.at[t, slot], device
        )

    mine = half == h.core
    for t in range(2):
        for x in range(XS):
            src, dst = stages[t][:2]

            @pl.when(jnp.logical_not(mine & (h.x == x)))
            def _():
                shard(t, x).start()

            @pl.when(mine & (h.x == x))
            def _():
                pltpu.make_async_copy(src.at[x], dst.at[slot], s1_r.at[t, slot]).start()

    def send_in(c, i):
        v, device = h.view_peer(*PEERS[i])
        return remote(
            pieces.at[v * 2 + c], xin.at[c, h.view], in_s.at[c, i], in_r.at[c, i], device
        )

    for c in range(2):
        for i in range(15):
            send_in(c, i).start()
        xin[c, h.view] = pieces[h.view * 2 + c]

    def put_together(t):
        dst, width = stages[t][1:]
        for s in range(4):
            pltpu.make_async_copy(dst.at[s], dst.at[s], s1_r.at[t, s]).wait()
            r32[20 * s : 20 * s + 20, 0:width] = dst[s, 0:20, :].astype(F32)
        rows = pl.ds(pl.multiple_of((h.yh * 2 + h.core) * ROWS, 16), ROWS)
        a, b = ((wqa, wqb), (woa, wob))[t]
        n = a.shape[2]
        for p in range(a.shape[0]):
            a[p, rows] = r32[:, n * p : n * (p + 1)].astype(BF)
        b[h.x, rows] = r32[:, width - GROUP : width].astype(BF)

    qa = Gather(h, wqa, False, sems[0:6])
    qb = Gather(h, wqb, True, sems[6:12])
    oa = Gather(h, woa, False, sems[12:18])
    ob = Gather(h, wob, True, sems[18:24])
    sqa, sqb, soa, sob = qa.steps(), qb.steps(), oa.steps(), ob.steps()

    put_together(0)
    advance(sqb, sqa)
    put_together(1)
    advance(sqb, sqa, times=2)
    advance(sob, soa)
    advance(sqb, sqa)
    advance(sqb, times=4)
    qa.arrive()
    qb.arrive()

    def project(c):
        for i in range(15):
            send_in(c, i).wait_recv()
        wide = xin[c].reshape(256, C).astype(F32)
        scale = lax.rsqrt(jnp.mean(wide * wide, axis=-1, keepdims=True) + 1e-06)
        normed = (wide * scale * gain[...].reshape(1, C)).astype(BF)
        tiles = [(256 * p, wqa[p]) for p in range(4)]
        tiles += [(1024, wqb[0]), (1408, wqb[1]), (1792, wqb[2, :, 0:128])]
        for at, w in tiles:
            qkv[c, :, at : at + w.shape[1]] = jnp.dot(
                normed, w, preferred_element_type=F32
            ).astype(BF)

    low = lax.broadcasted_iota(jnp.int32, (256, 128), 1) < 64

    def attend(c, s):
        q = qkv[c, :, 128 * s : 128 * (s + 1)]
        k = qkv[c, :, 640 + 128 * s : 640 + 128 * (s + 1)]
        v = qkv[c, :, 1280 + 128 * s : 1280 + 128 * (s + 1)]
        v = jnp.concatenate([v, jnp.ones_like(v)], axis=1)
        parts = []
        for e in range(2):
            qe = jnp.where(low if e == 0 else jnp.logical_not(low), q, jnp.zeros_like(q))
            scores = lax.dot_general(
                qe, k, (((1,), (1,)), ((), ())), preferred_element_type=F32
            )
            scores = scores * 0.125 - slope[2 * s + e] * dist[...]
            top = jnp.max(scores, axis=-1, keepdims=True)
            weights = jnp.exp(scores - top).astype(BF)
            o = jnp.dot(weights, v, preferred_element_type=F32)
            parts.append(o[:, 0:128] / o[:, 128:256])
        mix[c, :, 128 * s : 128 * (s + 1)] = jnp.where(low, parts[0], parts[1]).astype(BF)

    def halo(c, side):
        dst = (hright, hleft)[side]
        return remote(
            hsend.at[c, side], dst.at[c], halo_s.at[c, side], halo_r.at[c, side],
            h.frame_peer((-1, 1)[side]),
        )

    taps_of = (
        lambda: (woa[0], wob[0, :, 0:256]),
        lambda: (wob[0, :, 256:384], wob[1], wob[2, :, 0:128]),
        lambda: (wob[2, :, 128:384], wob[3]),
        lambda: (wqb[2, :, 128:384], wqb[3]),
    )

    def times(a, t):
        return jnp.concatenate(
            [jnp.dot(a, w, preferred_element_type=F32) for w in taps_of[t]()], axis=1
        )

    def add(c):
        wide = xin[c].reshape(256, C).astype(F32)
        hidden = (wide + times(mix[c], 3)).astype(BF)
        hid[c] = hidden
        split = hidden.astype(F32).reshape(16, 2, 8, C)
        for side in range(2):
            hsend[c, side] = split[:, side].reshape(128, C).astype(BF)
            halo(c, side).start()

    def convolve(c):
        for side in range(2):
            halo(c, side).wait_recv()
        wide = hid[c].astype(F32)
        split = wide.reshape(16, 2, 8, C)
        before = hleft[c].astype(F32).reshape(16, 8, C)
        after = hright[c].astype(F32).reshape(16, 8, C)
        before = jnp.where(h.frame == 0, 0.0, before)
        after = jnp.where(h.frame == 31, 0.0, after)
        taps = (
            jnp.stack([before, split[:, 0]], axis=1).reshape(256, C).astype(BF),
            hid[c],
            jnp.stack([split[:, 1], after], axis=1).reshape(256, C).astype(BF),
        )
        for t in range(3):
            wide = wide + times(taps[t], t)
        outb[c] = wide.astype(BF).reshape(16, 16, C)
        for i in range(15):
            send_out(c, i).start()
        back[c, h.view] = outb[c, h.view]

    def send_out(c, i):
        v, device = h.view_peer(*PEERS[i])
        return remote(
            outb.at[c, v], back.at[c, h.view], out_s.at[c, i], out_r.at[c, i], device
        )

    project(0)
    advance(sob, soa)
    for k in range(5):
        attend(0, k)
    add(0)
    advance(sob, soa)
    project(1)
    for k in range(5):
        attend(1, k)
    add(1)
    advance(sob, soa)
    advance(sob, times=4)
    oa.arrive()
    ob.arrive()
    convolve(0)
    convolve(1)

    for g in (qa, qb, oa, ob):
        g.drain()
    for t in range(2):
        for x in range(XS):
            @pl.when(jnp.logical_not(mine & (h.x == x)))
            def _():
                shard(t, x).wait_send()
    for c in range(2):
        for side in range(2):
            halo(c, side).wait_send()
        for i in range(15):
            send_in(c, i).wait_send()
    for c in range(2):
        for i in range(15):
            send_out(c, i).wait_recv()
    both = [back[c].astype(F32).reshape(16, 2, 8, C) for c in range(2)]
    for f in range(2):
        out[0, f] = jnp.stack([b[:, f] for b in both], axis=1).reshape(PIX, C).astype(BF)
    for c in range(2):
        for i in range(15):
            send_out(c, i).wait_send()


def per_device(latents, norm_gain, qkv_weight, out_weight, conv_weight, view_slope):
    vmem = pl.BlockSpec(memory_space=pltpu.VMEM)
    dma = pltpu.SemaphoreType.DMA
    scratch = [
        pltpu.VMEM((32, 16, C), BF),
        pltpu.VMEM((2, 16, 16, C), BF),
        pltpu.VMEM((2, 16, 16, C), BF),
        pltpu.VMEM((2, 16, 16, C), BF),
        pltpu.VMEM((256, 256), F32),
        pltpu.VMEM((4, C, QA // 4), BF),
        pltpu.VMEM((XS, C, GROUP), BF),
        pltpu.VMEM((1, C, OA), BF),
        pltpu.VMEM((XS, C, GROUP), BF),
        pltpu.VMEM((XS, 32, QA + GROUP), BF),
        pltpu.VMEM((XS, 32, OA + GROUP), BF),
        pltpu.VMEM((4, 32, QA + GROUP), BF),
        pltpu.VMEM((4, 32, OA + GROUP), BF),
        pltpu.VMEM((ROWS, QA + GROUP), F32),
        pltpu.VMEM((2, 256, 3 * C), BF),
        pltpu.VMEM((2, 256, C), BF),
        pltpu.VMEM((2, 256, C), BF),
        pltpu.VMEM((2, 2, 128, C), BF),
        pltpu.VMEM((2, 128, C), BF),
        pltpu.VMEM((2, 128, C), BF),
        dma((2, 15)), dma((2, 15)), dma((2, 15)), dma((2, 15)),
        dma((2, 2)), dma((2, 2)), dma((2, 4)), dma((2, 4)),
    ]
    for count, across in ((4, False), (XS, True), (1, False), (XS, True)):
        scratch += Gather.sems(count, across)
    return pl.pallas_call(
        kernel,
        out_shape=jax.ShapeDtypeStruct(latents.shape, latents.dtype),
        in_specs=[vmem] * 5 + [pl.BlockSpec(memory_space=pltpu.SMEM)],
        out_specs=vmem,
        scratch_shapes=scratch,
        compiler_params=pltpu.CompilerParams(
            collective_id=0, has_side_effects=True, vmem_limit_bytes=56 * 1024 * 1024
        ),
        cost_estimate=pl.CostEstimate(
            flops=4 * 10**9, bytes_accessed=2 * 10**6, transcendentals=10**6
        ),
    )(latents, norm_gain, qkv_weight, out_weight, conv_weight, view_slope)


def solution(mesh):
    in_specs = (
        P("view", "frame", None, None),
        P(),
        P("frame", None),
        P("frame", None),
        P(None, "frame", None),
        P(),
    )
    return jax.shard_map(
        per_device,
        mesh=mesh,
        in_specs=in_specs,
        out_specs=P("view", "frame", None, None),
        check_vma=False,
    )
```

time: 158 us -> 81.7 us (0.52)
  the two profiles are of different devices: /device:TPU:56 before, /device:TPU:1 now
where the time goes in v2:
time: 81.7 us; the launch traced here: 81.5 us
  Pallas kernels  79.5 us (97%)
  local copies, waits for them, and re-layouts  1.98 us (2%)
    pallas_call x1, Pallas kernels, per_device(): pl.pallas_call(kernel, out_shape=jax.ShapeDtypeStruct(latents.shape, late...  79.5 us
    unnamed x1, local copies, waits for them, and re-layouts  1.98 us

profile of v2, /device:TPU:1, one launch (start us, length us, event | category | flops | bytes accessed | tf_op | source)
XLA Modules:
  0.0 81.5 jit_solution(484161391172000651)
XLA Ops:
  0.0 79.5 %shard_map.64 = bf16[1,2,256,640]{3,2,1,0:T(8,128)(2,1)} custom-call(bf16[1,2,256,640]{3,2,1,0:T(8,128)(2,1)} %lat.1, f32[640]{0:T(1024)} %gain.1, bf16[20,1920]{1,0:T(8,128)(2,1)} %qsh.1, bf16[20,640]{1,0:T(8,128)(2,1)} %osh.1, bf16[3,20,640]{2,1,0:T(8,128)(2,1)} %csh.1, f32[10]{0:T(128)} %slope.1), custom_call_target="tpu_custom_call" | custom-call | flops 4000000000 | bytes 2000000 | tf_op jit(solution)/shard_map/pallas_call | solution.py:403
  79.5 2.0 %copy.8 = bf16[1,2,256,640]{3,2,1,0:T(8,128)(2,1)} copy(bf16[1,2,256,640]{3,2,1,0:T(8,128)(2,1)} %shard_map.64) | data formatting | bytes 1310720

commit v3 on v2

--- a/solution.py
+++ b/solution.py
@@ -8,10 +8,9 @@
 ZS, YLS, XS, YHS = 8, 2, 4, 4
 VIEWS, PIX, C, HEADS = 16, 256, 640, 10
 ROWS = 80
-QA, OA, GROUP = 1024, 384, 384
+CUT = 48
+QW, OW, SPLIT = 640, 512, 256
 PEERS = [(dy, dz) for dz in (4, 3, 5, 2, 6, 1, 7, 0) for dy in (0, 1) if (dy, dz) != (0, 0)]
-XSTEPS = (1, -1, 2)
-XFROM = (3, 1, 2)
 BF, F32 = jnp.bfloat16, jnp.float32
 
 
@@ -55,16 +54,16 @@
 class Gather:
     def __init__(self, here, buf, across, sems):
         self.h, self.buf, self.across = here, buf, across
-        self.count = buf.shape[0]
         self.side = 2 * here.yl - 1
         (self.ys, self.yr, self.xs, self.xr, self.ss, self.sr) = sems
 
-    def piece(self, b, p):
-        row = pl.multiple_of((((b + 8) % YHS) * 2 + self.h.core) * ROWS, 16)
-        return self.buf.at[p, pl.ds(row, ROWS)]
-
-    def copy(self, b, p, send, recv, device):
-        ref = self.piece(b, p)
+    def piece(self, b, p, part):
+        start, rows = part
+        row = pl.multiple_of((((b + 8) % YHS) * 2 + self.h.core) * ROWS + start, 16)
+        return self.buf.at[p, pl.ds(row, rows)]
+
+    def copy(self, b, p, send, recv, device, part=(0, ROWS)):
+        ref = self.piece(b, p, part)
         return remote(ref, ref, send, recv, device)
 
     def hop(self, k, i, b, p):
@@ -72,58 +71,90 @@
         return self.copy(b, p, self.ys.at[k, i], self.yr.at[k, i], self.h.y_peer(d))
 
     def to_sibling(self, b, p):
-        i = ((b + 8) % YHS) * self.count + p
+        i = ((b + 8) % YHS) * XS + p
         self.copy(b, p, self.ss.at[i], self.sr.at[i], self.h.sibling()).start()
 
     def pass_on(self, k, b, p):
         if self.across:
-            for i, d in enumerate(XSTEPS):
-                i += 3 * k
-                self.copy(b, p, self.xs.at[i], self.xr.at[i], self.h.x_peer(d)).start()
+            for i in range(2):
+                self.turn(i, k, b, 0).start()
         self.to_sibling(b, p)
+
+    def turn(self, i, k, b, rel):
+        part = ((0, ROWS), (0, ROWS), (0, CUT), (CUT, ROWS - CUT))[i]
+        device = self.h.x_peer((1, -1)[i % 2])
+        p = (self.h.x + rel) % XS
+        return self.copy(b, p, self.xs.at[i, k], self.xr.at[i, k], device, part)
+
+    def near(self, k, b):
+        for i, rel in enumerate((3, 1)):
+            self.turn(i, k, b, rel).wait_recv()
+            self.turn(2 + i, k, b, rel).start()
+            self.to_sibling(b, (self.h.x + rel) % XS)
+
+    def far(self, k, b):
+        for i in range(2, 4):
+            self.turn(i, k, b, 2).wait_recv()
+        self.to_sibling(b, (self.h.x + 2) % XS)
+
+    def direct(self, i, rel):
+        device = self.h.x_peer((1, -1, 2)[i])
+        p = (self.h.x + rel) % XS
+        return self.copy(self.h.yh, p, self.xs.at[i, 0], self.xr.at[i, 0], device)
 
     def steps(self):
         h = self.h
-        own = [h.x] if self.across else range(self.count)
+        own = [h.x] if self.across else [(h.x + rel) % XS for rel in (0, 3, 1, 2)]
         blocks = (h.yh + self.side, h.yh - self.side, h.yh + 2)
-        for i, p in enumerate(own):
-            self.hop(0, i, h.yh, p).start()
-        for p in own:
-            self.pass_on(0, h.yh, p)
+        self.hop(0, 0, h.yh, h.x).start()
+        if not self.across:
+            for i in range(3):
+                self.direct(i, 0).start()
+        self.pass_on(0, h.yh, h.x)
         yield
+        if not self.across:
+            for i, rel in enumerate((3, 1, 2)):
+                self.direct(i, rel).wait_recv()
+                self.hop(0, i + 1, h.yh, own[i + 1]).start()
+                self.to_sibling(h.yh, own[i + 1])
+            yield
         for k in range(3):
             for i, p in enumerate(own):
                 self.hop(k, i, blocks[k], p).wait_recv()
                 if k < 2:
                     self.hop(k + 1, i, blocks[k], p).start()
                 self.pass_on(k + 1, blocks[k], p)
+            if self.across:
+                self.near(k, ((h.yh,) + blocks)[k])
             yield
         if self.across:
+            self.near(3, blocks[2])
+            yield
             for k, b in enumerate((h.yh,) + blocks):
-                for i, rel in enumerate(XFROM):
-                    p = (h.x + rel) % XS
-                    i += 3 * k
-                    self.copy(b, p, self.xs.at[i], self.xr.at[i], h.x_peer(1)).wait_recv()
-                    self.to_sibling(b, p)
-                yield
+                self.far(k, b)
+            yield
 
     def arrive(self):
-        for i in range(YHS * self.count):
+        for i in range(YHS * XS):
             self.copy(0, 0, self.ss.at[i], self.sr.at[i], self.h.sibling()).wait_recv()
 
     def drain(self):
-        own = 1 if self.across else self.count
+        own = 1 if self.across else XS
         waits = [self.ys.at[k, i] for k in range(3) for i in range(own)]
-        waits += [self.ss.at[i] for i in range(YHS * self.count)]
-        if self.across:
-            waits += [self.xs.at[i] for i in range(12)]
+        waits += [self.ss.at[i] for i in range(YHS * XS)]
         for sem in waits:
             self.copy(0, 0, sem, self.sr.at[0], self.h.sibling()).wait_send()
+        if self.across:
+            for i in range(4):
+                for k in range(4):
+                    self.turn(i, k, 0, 0).wait_send()
+        else:
+            for i in range(3):
+                self.direct(i, 0).wait_send()
 
     @staticmethod
-    def sems(count, across):
-        own = 1 if across else count
-        shapes = ((3, own), (3, own), (12,), (12,), (YHS * count,), (YHS * count,))
+    def sems():
+        shapes = ((3, 4), (3, 4), (4, 4), (4, 4), (16,), (16,))
         return [pltpu.SemaphoreType.DMA(k) for k in shapes]
 
 
@@ -153,23 +184,17 @@
         pl.semaphore_signal(barrier, inc=1, device_id=p, device_id_type=pl.DeviceIdType.MESH)
 
     for x in range(XS):
-        first, last = QA + GROUP * x, QA + GROUP * (x + 1)
-        sq[x, 0:20, 0:QA] = qsh[:, 0:QA]
-        if first < 1920:
-            sq[x, 0:20, QA : QA + min(last, 1920) - first] = qsh[:, first : min(last, 1920)]
-        if last > 1920:
-            skip = max(first, 1920)
-            sq[x, 0:20, QA + skip - first :] = osh[:, skip - 1920 : last - 1920]
-        so[x, 0:20, 0:OA] = csh[0, :, 0:OA]
-        at, end = OA + GROUP * x, OA + GROUP * (x + 1)
+        sq[x, 0:20] = qsh[:, QW * x : QW * (x + 1)] if x < 3 else osh[...]
+        sq[x, 20:32] = jnp.zeros((12, QW), BF)
+        at, end = OW * x, min(OW * (x + 1), 3 * C)
         while at < end:
             t = at // C
             stop = min(end, C * (t + 1))
-            to = OA + at - (OA + GROUP * x)
-            so[x, 0:20, to : to + stop - at] = csh[t, :, at - C * t : stop - C * t]
+            so[x, 0:20, at - OW * x : stop - OW * x] = csh[t, :, at - C * t : stop - C * t]
             at = stop
-        sq[x, 20:32, :] = jnp.zeros((12, QA + GROUP), BF)
-        so[x, 20:32, :] = jnp.zeros((12, OA + GROUP), BF)
+        if end < OW * (x + 1):
+            so[x, 0:20, end - OW * x :] = jnp.zeros((20, OW * (x + 1) - end), BF)
+        so[x, 20:32] = jnp.zeros((12, OW), BF)
     both = [lat[0, f].astype(F32).reshape(32, 8, C) for f in range(2)]
     pieces[...] = jnp.stack(both, axis=1).reshape(32, 16, C).astype(BF)
     row = lax.broadcasted_iota(jnp.int32, (256, 256), 0)
@@ -182,7 +207,7 @@
 
     half = h.x // 2
     slot = (h.x % 2) * 2 + h.core
-    stages = ((sq, r1q, QA + GROUP), (so, r1o, OA + GROUP))
+    stages = ((sq, r1q, QW), (so, r1o, OW))
 
     def shard(t, x):
         src, dst = stages[t][:2]
@@ -222,10 +247,8 @@
             r32[20 * s : 20 * s + 20, 0:width] = dst[s, 0:20, :].astype(F32)
         rows = pl.ds(pl.multiple_of((h.yh * 2 + h.core) * ROWS, 16), ROWS)
         a, b = ((wqa, wqb), (woa, wob))[t]
-        n = a.shape[2]
-        for p in range(a.shape[0]):
-            a[p, rows] = r32[:, n * p : n * (p + 1)].astype(BF)
-        b[h.x, rows] = r32[:, width - GROUP : width].astype(BF)
+        a[h.x, rows] = r32[:, 0:SPLIT].astype(BF)
+        b[h.x, rows] = r32[:, SPLIT:width].astype(BF)
 
     qa = Gather(h, wqa, False, sems[0:6])
     qb = Gather(h, wqb, True, sems[6:12])
@@ -236,10 +259,15 @@
     put_together(0)
     advance(sqb, sqa)
     put_together(1)
-    advance(sqb, sqa, times=2)
     advance(sob, soa)
-    advance(sqb, sqa)
-    advance(sqb, times=4)
+    advance(sqa, sqb)
+    advance(sqa, sqb)
+    advance(soa, sob)
+    advance(sqa, sqb)
+    advance(soa, sob)
+    advance(sqa, sqb)
+    advance(soa, sob)
+    advance(sqb)
     qa.arrive()
     qb.arrive()
 
@@ -249,8 +277,7 @@
         wide = xin[c].reshape(256, C).astype(F32)
         scale = lax.rsqrt(jnp.mean(wide * wide, axis=-1, keepdims=True) + 1e-06)
         normed = (wide * scale * gain[...].reshape(1, C)).astype(BF)
-        tiles = [(256 * p, wqa[p]) for p in range(4)]
-        tiles += [(1024, wqb[0]), (1408, wqb[1]), (1792, wqb[2, :, 0:128])]
+        tiles = [(QW * p + at, w[p]) for p in range(3) for at, w in ((0, wqa), (SPLIT, wqb))]
         for at, w in tiles:
             qkv[c, :, at : at + w.shape[1]] = jnp.dot(
                 normed, w, preferred_element_type=F32
@@ -284,10 +311,10 @@
         )
 
     taps_of = (
-        lambda: (woa[0], wob[0, :, 0:256]),
-        lambda: (wob[0, :, 256:384], wob[1], wob[2, :, 0:128]),
-        lambda: (wob[2, :, 128:384], wob[3]),
-        lambda: (wqb[2, :, 128:384], wqb[3]),
+        lambda: (woa[0], wob[0], woa[1, :, 0:128]),
+        lambda: (woa[1, :, 128:256], wob[1], woa[2]),
+        lambda: (wob[2], woa[3], wob[3, :, 0:128]),
+        lambda: (wqa[3], wqb[3]),
     )
 
     def times(a, t):
@@ -332,17 +359,15 @@
         )
 
     project(0)
-    advance(sob, soa)
+    advance(soa, sob)
     for k in range(5):
         attend(0, k)
     add(0)
-    advance(sob, soa)
+    advance(sob)
     project(1)
     for k in range(5):
         attend(1, k)
     add(1)
-    advance(sob, soa)
-    advance(sob, times=4)
     oa.arrive()
     ob.arrive()
     convolve(0)
@@ -380,15 +405,15 @@
         pltpu.VMEM((2, 16, 16, C), BF),
         pltpu.VMEM((2, 16, 16, C), BF),
         pltpu.VMEM((256, 256), F32),
-        pltpu.VMEM((4, C, QA // 4), BF),
-        pltpu.VMEM((XS, C, GROUP), BF),
-        pltpu.VMEM((1, C, OA), BF),
-        pltpu.VMEM((XS, C, GROUP), BF),
-        pltpu.VMEM((XS, 32, QA + GROUP), BF),
-        pltpu.VMEM((XS, 32, OA + GROUP), BF),
-        pltpu.VMEM((4, 32, QA + GROUP), BF),
-        pltpu.VMEM((4, 32, OA + GROUP), BF),
-        pltpu.VMEM((ROWS, QA + GROUP), F32),
+        pltpu.VMEM((XS, C, SPLIT), BF),
+        pltpu.VMEM((XS, C, QW - SPLIT), BF),
+        pltpu.VMEM((XS, C, SPLIT), BF),
+        pltpu.VMEM((XS, C, OW - SPLIT), BF),
+        pltpu.VMEM((XS, 32, QW), BF),
+        pltpu.VMEM((XS, 32, OW), BF),
+        pltpu.VMEM((4, 32, QW), BF),
+        pltpu.VMEM((4, 32, OW), BF),
+        pltpu.VMEM((ROWS, QW), F32),
         pltpu.VMEM((2, 256, 3 * C), BF),
         pltpu.VMEM((2, 256, C), BF),
         pltpu.VMEM((2, 256, C), BF),
@@ -398,8 +423,8 @@
         dma((2, 15)), dma((2, 15)), dma((2, 15)), dma((2, 15)),
         dma((2, 2)), dma((2, 2)), dma((2, 4)), dma((2, 4)),
     ]
-    for count, across in ((4, False), (XS, True), (1, False), (XS, True)):
-        scratch += Gather.sems(count, across)
+    for _ in range(4):
+        scratch += Gather.sems()
     return pl.pallas_call(
         kernel,
         out_shape=jax.ShapeDtypeStruct(latents.shape, latents.dtype),

time: 81.7 us -> 74.9 us (0.917); the launches traced: 81.5 us -> 73.8 us
  Pallas kernels: 79.5 us -> 71.8 us
    pallas_call x1, Pallas kernels: 79.5 us -> 71.8 us  [per_device(): pl.pallas_call(kernel, out_shape=jax.ShapeDtypeStruct(latents.shape, late...]
where the time goes in v3:
time: 74.9 us; the launch traced here: 73.8 us
  Pallas kernels  71.8 us (96%)
  local copies, waits for them, and re-layouts  1.98 us (3%)
    pallas_call x1, Pallas kernels, per_device(): pl.pallas_call(kernel, out_shape=jax.ShapeDtypeStruct(latents.shape, late...  71.8 us
    unnamed x1, local copies, waits for them, and re-layouts  1.98 us

profile of v3, /device:TPU:1, one launch (start us, length us, event | category | flops | bytes accessed | tf_op | source)
XLA Modules:
  0.0 73.8 jit_solution(2874764858445690853)
XLA Ops:
  0.0 71.8 %shard_map.64 = bf16[1,2,256,640]{3,2,1,0:T(8,128)(2,1)} custom-call(bf16[1,2,256,640]{3,2,1,0:T(8,128)(2,1)} %lat.1, f32[640]{0:T(1024)} %gain.1, bf16[20,1920]{1,0:T(8,128)(2,1)} %qsh.1, bf16[20,640]{1,0:T(8,128)(2,1)} %osh.1, bf16[3,20,640]{2,1,0:T(8,128)(2,1)} %csh.1, f32[10]{0:T(128)} %slope.1), custom_call_target="tpu_custom_call" | custom-call | flops 4000000000 | bytes 2000000 | tf_op jit(solution)/shard_map/pallas_call | solution.py:428
  71.9 2.0 %copy.8 = bf16[1,2,256,640]{3,2,1,0:T(8,128)(2,1)} copy(bf16[1,2,256,640]{3,2,1,0:T(8,128)(2,1)} %shard_map.64) | data formatting | bytes 1310720

commit v4 on v3

--- a/solution.py
+++ b/solution.py
@@ -76,24 +76,27 @@
 
     def pass_on(self, k, b, p):
         if self.across:
-            for i in range(2):
+            for i in range(3 if k == 3 else 2):
                 self.turn(i, k, b, 0).start()
         self.to_sibling(b, p)
 
     def turn(self, i, k, b, rel):
         part = ((0, ROWS), (0, ROWS), (0, CUT), (CUT, ROWS - CUT))[i]
         device = self.h.x_peer((1, -1)[i % 2])
+        if i == 2 and k == 3:
+            part, device = (0, ROWS), self.h.x_peer(2)
         p = (self.h.x + rel) % XS
         return self.copy(b, p, self.xs.at[i, k], self.xr.at[i, k], device, part)
 
     def near(self, k, b):
         for i, rel in enumerate((3, 1)):
             self.turn(i, k, b, rel).wait_recv()
-            self.turn(2 + i, k, b, rel).start()
+            if k < 3:
+                self.turn(2 + i, k, b, rel).start()
             self.to_sibling(b, (self.h.x + rel) % XS)
 
     def far(self, k, b):
-        for i in range(2, 4):
+        for i in range(2, 3 if k == 3 else 4):
             self.turn(i, k, b, 2).wait_recv()
         self.to_sibling(b, (self.h.x + 2) % XS)
 
@@ -146,7 +149,7 @@
             self.copy(0, 0, sem, self.sr.at[0], self.h.sibling()).wait_send()
         if self.across:
             for i in range(4):
-                for k in range(4):
+                for k in range(3 if i == 3 else 4):
                     self.turn(i, k, 0, 0).wait_send()
         else:
             for i in range(3):
@@ -179,7 +182,8 @@
                 partners.append(
                     (h.view, h.yh * 8 + ((h.x + dx) % XS) * 2 + (h.core + dc) % 2)
                 )
-    partners += [h.y_peer(1), h.y_peer(-1), h.frame_peer(1), h.frame_peer(-1)]
+    partners += [h.y_peer(d) for d in (1, -1)]
+    partners += [h.frame_peer(1), h.frame_peer(-1)]
     for p in partners:
         pl.semaphore_signal(barrier, inc=1, device_id=p, device_id_type=pl.DeviceIdType.MESH)
 

time: 74.9 us -> 74.1 us (0.989); the launches traced: 73.8 us -> 73.9 us
  no operation moved by 1% of the time
where the time goes in v4:
time: 74.1 us; the launch traced here: 73.9 us
  Pallas kernels  71.9 us (97%)
  local copies, waits for them, and re-layouts  1.98 us (3%)
    pallas_call x1, Pallas kernels, per_device(): pl.pallas_call(kernel, out_shape=jax.ShapeDtypeStruct(latents.shape, late...  71.9 us
    unnamed x1, local copies, waits for them, and re-layouts  1.98 us

profile of v4, /device:TPU:1, one launch (start us, length us, event | category | flops | bytes accessed | tf_op | source)
XLA Modules:
  0.0 73.9 jit_solution(11901690160242380513)
XLA Ops:
  0.0 71.9 %shard_map.64 = bf16[1,2,256,640]{3,2,1,0:T(8,128)(2,1)} custom-call(bf16[1,2,256,640]{3,2,1,0:T(8,128)(2,1)} %lat.1, f32[640]{0:T(1024)} %gain.1, bf16[20,1920]{1,0:T(8,128)(2,1)} %qsh.1, bf16[20,640]{1,0:T(8,128)(2,1)} %osh.1, bf16[3,20,640]{2,1,0:T(8,128)(2,1)} %csh.1, f32[10]{0:T(128)} %slope.1), custom_call_target="tpu_custom_call" | custom-call | flops 4000000000 | bytes 2000000 | tf_op jit(solution)/shard_map/pallas_call | solution.py:432
  71.9 2.0 %copy.8 = bf16[1,2,256,640]{3,2,1,0:T(8,128)(2,1)} copy(bf16[1,2,256,640]{3,2,1,0:T(8,128)(2,1)} %shard_map.64) | data formatting | bytes 1310720

commit v5 on v4

--- a/solution.py
+++ b/solution.py
@@ -263,8 +263,8 @@
     put_together(0)
     advance(sqb, sqa)
     put_together(1)
+    advance(sqa, sqb)
     advance(sob, soa)
-    advance(sqa, sqb)
     advance(sqa, sqb)
     advance(soa, sob)
     advance(sqa, sqb)

time: 74.1 us -> 74.2 us (level)
  no operation moved by 1% of the time
where the time goes in v5:
time: 74.2 us; the launch traced here: 73.3 us
  Pallas kernels  71.4 us (96%)
  local copies, waits for them, and re-layouts  1.98 us (3%)
    pallas_call x1, Pallas kernels, per_device(): pl.pallas_call(kernel, out_shape=jax.ShapeDtypeStruct(latents.shape, late...  71.4 us
    unnamed x1, local copies, waits for them, and re-layouts  1.98 us

profile of v5, /device:TPU:1, one launch (start us, length us, event | category | flops | bytes accessed | tf_op | source)
XLA Modules:
  0.0 73.3 jit_solution(8654453465511444138)
XLA Ops:
  0.0 71.4 %shard_map.64 = bf16[1,2,256,640]{3,2,1,0:T(8,128)(2,1)} custom-call(bf16[1,2,256,640]{3,2,1,0:T(8,128)(2,1)} %lat.1, f32[640]{0:T(1024)} %gain.1, bf16[20,1920]{1,0:T(8,128)(2,1)} %qsh.1, bf16[20,640]{1,0:T(8,128)(2,1)} %osh.1, bf16[3,20,640]{2,1,0:T(8,128)(2,1)} %csh.1, f32[10]{0:T(128)} %slope.1), custom_call_target="tpu_custom_call" | custom-call | flops 4000000000 | bytes 2000000 | tf_op jit(solution)/shard_map/pallas_call | solution.py:432
  71.4 2.0 %copy.8 = bf16[1,2,256,640]{3,2,1,0:T(8,128)(2,1)} copy(bf16[1,2,256,640]{3,2,1,0:T(8,128)(2,1)} %shard_map.64) | data formatting | bytes 1310720
